TPU v7x, 256 devices: a whole 4x4x8 slice. The times are simulated.
256 devices in a mesh: frame: 64 (over y, z, x_lo), mp: 4 (over x_hi, core).
Axes of the slice: x: 4 (x_hi: 2, x_lo: 2; x = x_hi * 2 + x_lo), y: 4, z: 8, core: 2. Of those that a mesh axis runs over, the one named last changes fastest.
Arguments:
- latents: bfloat16 [512, 96, 3072], P(('frame', 'mp')), may hold values from -6 to 6
- levels: int32 [64], P('frame'), may hold values from 0 to 49, as said below
- window_reach: int32 [64], P('frame'), may hold values from 1 to 2, as said below
- query_gain: float32 [128], replicated, may hold values from 1.2 to 5
- key_gain: float32 [128], replicated, may hold values from 1.2 to 5
- qkv_weight: bfloat16 [3072, 4608], P('mp'), may hold values from -0.109375 to 0.109375
- out_weight: bfloat16 [1536, 3072], P('mp'), may hold values from -0.15625 to 0.15625
- mod_weight: bfloat16 [256, 9216], P(None, 'mp'), may hold values from -0.375 to 0.375
Outputs:
- queue_next: bfloat16 [512, 96, 3072], P(('frame', 'mp'))
- velocity: bfloat16 [512, 96, 3072], P(('frame', 'mp'))
Inputs may be any that keep to these rules, and one draw needn't show every extreme that they name: `levels`: some slot has level 49 and some has 0. `window_reach`: some slot has reach 2 and some has 1.
All inputs are finite; a program needn't handle non-finite values.
Results may differ from a plain program's by a relative error of at most 0.027.
Values may be sent and summed in bfloat16 or wider, within the bound.
A program may use at most 128 MiB of HBM per device.

v0:
```python
import math

import jax
import jax.numpy as jnp
from jax import lax
from jax.sharding import PartitionSpec as P

HEAD = 128
FREQ = 256
NOISE_LEVELS = 50
REACH_LIMIT = 2


flow_shift = 7.0


def extended(cells, sides, width):
    for axis, dim in sides:
        count = lax.axis_size(axis)
        ends = count - 1
        head = lax.slice_in_dim(cells, 0, width, axis=dim)
        tail = lax.slice_in_dim(cells, cells.shape[dim] - width, cells.shape[dim], axis=dim)
        cells = jnp.concatenate(
            [
                lax.ppermute(tail, axis, [(i, (i + 1) % count) for i in range(ends)]),
                cells,
                lax.ppermute(head, axis, [((i + 1) % count, i) for i in range(ends)]),
            ],
            axis=dim,
        )
    return cells


def from_behind(value, axis, steps):
    count = lax.axis_size(axis)
    pairs = [(source, (source + steps) % count) for source in range(count)]
    return lax.ppermute(value, axis, pairs)


def flow_sigma(position):
    return flow_shift * position / (1.0 + (flow_shift - 1.0) * position)


def level_terms(level_value):
    upper = (level_value + 1.0) / NOISE_LEVELS
    lower = level_value / NOISE_LEVELS
    sigma_now = flow_sigma(upper)
    step_size = sigma_now - flow_sigma(lower)
    half_count = FREQ // 2
    index_row = jnp.arange(half_count).astype(jnp.float32)
    frequency = jnp.exp(-math.log(10000.0) * index_row / half_count)
    angles = 1000.0 * sigma_now[:, None] * frequency[None, :]
    embedded = jnp.concatenate([jnp.cos(angles), jnp.sin(angles)], axis=-1)
    return (jax.nn.silu(embedded).astype(jnp.bfloat16), step_size)


def head_norm(values, gain):
    widened = values.astype(jnp.float32)
    meansq = jnp.mean(widened * widened, axis=-1, keepdims=True)
    return (widened * lax.rsqrt(meansq + 1e-06) * gain).astype(jnp.bfloat16)


def modulate(token_rows, shift_row, scale_row):
    widened = token_rows.astype(jnp.float32)
    center = jnp.mean(widened, axis=-1, keepdims=True)
    spread = jnp.mean((widened - center) * (widened - center), axis=-1, keepdims=True)
    normed = (widened - center) * lax.rsqrt(spread + 1e-06)
    return (normed * (1.0 + scale_row) + shift_row).astype(jnp.bfloat16)


def per_device(
    latents, levels, window_reach, query_gain, key_gain, qkv_weight, out_weight, mod_weight
):
    frames, spatial, width = latents.shape
    row_count = frames * spatial
    inner = out_weight.shape[0] * lax.axis_size("mp")
    heads = inner // HEAD
    activity, step_size = level_terms(levels.astype(jnp.float32))
    own_part = jnp.dot(activity, mod_weight, preferred_element_type=jnp.float32)
    modulation = lax.all_gather(own_part, "mp", axis=1, tiled=True)[0]
    token_rows = latents.reshape(row_count, width)
    hidden = modulate(token_rows, modulation[:width], modulation[width : 2 * width])
    picked = hidden
    summed = jnp.dot(
        picked,
        lax.all_gather(qkv_weight, "mp", axis=0, tiled=True),
        preferred_element_type=jnp.float32,
    )
    projected = summed.astype(jnp.bfloat16)
    queries = head_norm(projected[:, :inner].reshape(row_count, heads, HEAD), query_gain)
    key_rows = head_norm(projected[:, inner : 2 * inner].reshape(row_count, heads, HEAD), key_gain)
    key_value = jnp.concatenate(
        [key_rows.reshape(row_count, inner), projected[:, 2 * inner :]], axis=-1
    )
    key_value = key_value.reshape(frames, spatial, 2 * inner)
    widened = extended(key_value, ((("frame", "mp"), 0),), REACH_LIMIT)
    key_count = (frames + 2 * REACH_LIMIT) * spatial
    key_block = widened[:, :, :inner].reshape(key_count, heads, HEAD)
    value_block = widened[:, :, inner:].reshape(key_count, heads, HEAD)
    first_frame = lax.axis_index(("frame", "mp")) * frames
    total_frames = frames * lax.axis_size(("frame", "mp"))
    query_frame = first_frame + jnp.arange(row_count, dtype=jnp.int32) // spatial
    key_frame = first_frame - REACH_LIMIT + jnp.arange(key_count, dtype=jnp.int32) // spatial
    valid = jnp.abs(key_frame[None, :] - query_frame[:, None]) <= window_reach[0]
    valid = valid & (key_frame >= 0)[None, :] & (key_frame < total_frames)[None, :]
    scores = jnp.einsum(
        "qhd,khd->hqk", queries, key_block, preferred_element_type=jnp.float32
    ) / math.sqrt(HEAD)
    scores = jnp.where(valid[None], scores, -jnp.inf)
    peak = jnp.max(scores, axis=-1, keepdims=True)
    raised = jnp.where(valid[None], jnp.exp(scores - peak), 0.0)
    weights = (raised / jnp.sum(raised, axis=-1, keepdims=True)).astype(jnp.bfloat16)
    mixed = jnp.einsum("hqk,khd->qhd", weights, value_block, preferred_element_type=jnp.float32)
    mixed = mixed.astype(jnp.bfloat16).reshape(row_count, inner)
    picked = mixed
    attended = jnp.dot(
        picked,
        lax.all_gather(out_weight, "mp", axis=0, tiled=True),
        preferred_element_type=jnp.float32,
    )
    base = token_rows.astype(jnp.float32)
    velocity_full = base + modulation[2 * width :] * attended
    stepped = (base - step_size * velocity_full).astype(jnp.bfloat16)
    queue_next = from_behind(stepped.reshape(frames, spatial, width), "frame", -1)
    return (queue_next, velocity_full.astype(jnp.bfloat16).reshape(frames, spatial, width))


def solution(mesh):
    return jax.shard_map(
        per_device,
        mesh=mesh,
        in_specs=(
            P(("frame", "mp"), None, None),
            P("frame"),
            P("frame"),
            P(),
            P(),
            P("mp", None),
            P("mp", None),
            P(None, "mp"),
        ),
        out_specs=(P(("frame", "mp"), None, None), P(("frame", "mp"), None, None)),
        check_vma=False,
    )
```

profile of v0, /device:TPU:0, one launch (start us, length us, event | category | flops | bytes accessed | tf_op | source)
XLA Modules:
  0.0 341.1 jit_solution(8361192376438013552)
XLA Ops:
  10.7 6.7 %all-gather.1 = f32[4,1,2304]{2,1,0:T(1,128)S(1)} all-gather(f32[1,1,2304]{2,1,0:T(1,128)S(1)} %convolution_bitcast_fusion), channel_id=2, replica_groups=mesh['frame'=64,'mp'=4] {'mp'}, dimensions={0}, use_global_device_ids=true | all-gather | bytes 46080 | tf_op jit(solution)/shard_map/all_gather | solution.py:80
  17.9 172.0 %all-gather.5.cloned.1.call-done = bf16[3072,4608]{1,0:T(8,128)(2,1)} async-done(((bf16[768,4608]{1,0:T(8,128)(2,1)}), bf16[3072,4608]{1,0:T(8,128)(2,1)}) %all-gather.5.cloned.1.call-update) | async-done | bytes 28311568 | tf_op jit(solution)/shard_map/all_gather | solution.py:86
  189.9 12.2 %convolution_convert_fusion = bf16[192,4608]{1,0:T(8,128)(2,1)S(1)} fusion(bf16[192,3072]{1,0:T(8,128)(2,1)S(1)} %fusion.10, bf16[3072,4608]{1,0:T(8,128)(2,1)} %all-gather.5.cloned.1.call-done), kind=kOutput, calls=%fused_computation.1 | convolution fusion | flops 5436702720 | bytes 31260672 | tf_op jit(solution)/shard_map/dot_general | solution.py:84
  202.1 1.2 copy-done.5
  203.3 1.1 convert_multiply_fusion.1
  204.4 1.6 mul.165
  206.7 2.5 slice_convert_fusion
  209.7 1.6 fusion.24
  212.1 1.2 pad_maximum_fusion.1
  213.3 3.5 %collective-permute-start = (bf16[2,96,3072]{2,1,0:T(8,128)(2,1)}, bf16[2,96,3072]{2,1,0:T(8,128)(2,1)}, u32[]{:S(2)}, u32[]{:S(2)}) collective-permute-start(bf16[2,96,3072]{2,1,0:T(8,128)(2,1)} %pad_maximum_fusion.1), channel_id=1, source_target_pairs={{0,1},{1,2},{2,3},{3,4},{4,5},{5,6},{6,7},{7,8},{8,9},{9,10},{10,1... | collective-permute-start | bytes 3538952 | tf_op jit(solution)/shard_map/ppermute | solution.py:25
  216.7 1.5 collective-permute-start.1
  219.8 1.5 reshape.225
  222.0 1.4 multiply_convert_fusion
  223.4 1.9 pad_maximum_fusion
  225.2 2.2 fusion.40
  227.4 4.3 %reshape.220 = bf16[576,12,128]{2,1,0:T(8,128)(2,1)} reshape(bf16[6,96,1536]{2,1,0:T(8,128)(2,1)} %get-tuple-element.2) | data formatting | bytes 3538944 | tf_op jit(solution)/shard_map/reshape | solution.py:98
  231.7 4.3 %reshape.219 = bf16[576,12,128]{2,1,0:T(8,128)(2,1)} reshape(bf16[6,96,1536]{2,1,0:T(8,128)(2,1)} %get-tuple-element.3) | data formatting | bytes 3538944 | tf_op jit(solution)/shard_map/reshape | solution.py:99
  236.0 3.1 fusion.15
  239.1 3.6 %fusion.42 = (f32[12,192]{1,0:T(8,128)S(1)}, f32[12,192,576]{2,1,0:T(8,128)S(1)}) fusion(f32[12,192,576]{2,1,0:T(8,128)S(1)} %fusion.15, pred[192,576]{1,0:T(8,128)(4,1)S(1)} %copy-done.8), kind=kOutput, calls=%fused_computation.75 | output fusion | flops 9290303 | bytes 10736640 | tf_op jit(solution)/shard_map/sub | solution.py:111
  242.7 2.0 fusion.20
  244.7 42.7 %all-gather.7.cloned.1.call-done = bf16[1536,3072]{1,0:T(8,128)(2,1)} async-done(((bf16[384,3072]{1,0:T(8,128)(2,1)}), bf16[1536,3072]{1,0:T(8,128)(2,1)}) %all-gather.7.cloned.1.call-update) | async-done | bytes 9437200 | tf_op jit(solution)/shard_map/all_gather | solution.py:118
  287.3 7.1 %fusion.41 = (bf16[192,3072]{1,0:T(8,128)(2,1)}, bf16[192,3072]{1,0:T(8,128)(2,1)S(1)}) fusion(f32[]{:T(128)} %bitcast.1, bf16[2,96,3072]{2,1,0:T(8,128)(2,1)S(1)} %copy-done.2, bf16[1536,3072]{1,0:T(8,128)(2,1)} %all-gather.7.cloned.1.call-done, bf16[12,24,8,128]{3,2,1,0:T(8,128)(2,1)S(1)} %fusion.20, f32[3072]{0:T(1024)S(1)} %bitcast.55, ...), kind=kOutput, calls=%fused_computation.74 | convolution fusion | flops 1816657920 | bytes 14757892 | tf_op jit(solution)/shard_map/dot_general | solution.py:116
  294.4 25.1 %collective-permute-start.2 = (bf16[2,96,3072]{2,1,0:T(8,128)(2,1)S(1)}, bf16[2,96,3072]{2,1,0:T(8,128)(2,1)S(1)}, u32[]{:S(2)}, u32[]{:S(2)}) collective-permute-start(bf16[2,96,3072]{2,1,0:T(8,128)(2,1)S(1)} %bitcast.56), channel_id=1, source_target_pairs={{0,252},{4,0},{8,4},{12,8},{16,12},{20,16},{24,20},{28,24},{32,28}... | collective-permute-start | bytes 3538952 | tf_op jit(solution)/shard_map/ppermute | solution.py:37
  319.5 13.7 %collective-permute-done.2 = bf16[2,96,3072]{2,1,0:T(8,128)(2,1)S(1)} collective-permute-done((bf16[2,96,3072]{2,1,0:T(8,128)(2,1)S(1)}, bf16[2,96,3072]{2,1,0:T(8,128)(2,1)S(1)}, u32[]{:S(2)}, u32[]{:S(2)}) %collective-permute-start.2) | collective-permute-done | bytes 1179680 | tf_op jit(solution)/shard_map/ppermute | solution.py:37
  (54 shorter events, 7.9 us)
Async XLA Ops:
  7.2 3.2 copy-start
  7.2 182.7 %all-gather.5.cloned.1.call-start = ((), (), s32[]{:S(2)}) async-start(), calls=%async_computation | async-start | bytes 35389440 | tf_op jit(solution)/shard_map/all_gather | solution.py:86
  7.9 1.6 copy-start.2
  7.9 279.4 %all-gather.7.cloned.1.call-start = ((), (), s32[]{:S(2)}) async-start(), calls=%async_computation.1 | async-start | bytes 11796480 | tf_op jit(solution)/shard_map/all_gather | solution.py:118
  8.7 8.7 %copy-start.9 = (f32[128]{0:T(128)S(1)}, f32[128]{0:T(128)}, u32[]{:S(2)}) copy-start(f32[128]{0:T(128)} %param.12) | copy-start | bytes 1540
  202.1 1.2 copy-start.5
  211.3 0.8 copy-start.3
  213.3 10.1 %collective-permute-start = (bf16[2,96,3072]{2,1,0:T(8,128)(2,1)}, bf16[2,96,3072]{2,1,0:T(8,128)(2,1)}, u32[]{:S(2)}, u32[]{:S(2)}) collective-permute-start(bf16[2,96,3072]{2,1,0:T(8,128)(2,1)} %pad_maximum_fusion.1), channel_id=1, source_target_pairs={{0,1},{1,2},{2,3},{3,4},{4,5},{5,6},{6,7},{7,8},{8,9},{9,10},{10,1... | collective-permute-start | bytes 3538952 | tf_op jit(solution)/shard_map/ppermute | solution.py:25
  216.7 6.6 %collective-permute-start.1 = (bf16[2,96,3072]{2,1,0:T(8,128)(2,1)}, bf16[2,96,3072]{2,1,0:T(8,128)(2,1)}, u32[]{:S(2)}, u32[]{:S(2)}) collective-permute-start(bf16[2,96,3072]{2,1,0:T(8,128)(2,1)} %pad_maximum_fusion.1), channel_id=1, source_target_pairs={{1,0},{2,1},{3,2},{4,3},{5,4},{6,5},{7,6},{8,7},{9,8},{10,9},{11,1... | collective-permute-start | bytes 3538952 | tf_op jit(solution)/shard_map/ppermute | solution.py:27
  219.8 2.2 copy-start.10
  222.0 1.4 copy-start.4
  231.7 4.3 %copy-start.6 = (bf16[192,12,128]{2,1,0:T(8,128)(2,1)S(1)}, bf16[192,12,128]{2,1,0:T(8,128)(2,1)}, u32[]{:S(2)}) copy-start(bf16[192,12,128]{2,1,0:T(8,128)(2,1)} %multiply_convert_fusion) | copy-start | bytes 1769476
  236.0 3.1 copy-start.8
  239.1 3.6 %copy-start.7 = (bf16[576,12,128]{2,1,0:T(8,128)(2,1)S(1)}, bf16[576,12,128]{2,1,0:T(8,128)(2,1)}, u32[]{:S(2)}) copy-start(bf16[576,12,128]{2,1,0:T(8,128)(2,1)} %reshape.219) | copy-start | bytes 5308420
  287.3 46.9 %copy-start.1 = (bf16[256,2304]{1,0:T(8,128)(2,1)S(1)}, bf16[256,2304]{1,0:T(8,128)(2,1)}, u32[]{:S(2)}) copy-start(bf16[256,2304]{1,0:T(8,128)(2,1)} %param.15) | copy-start | bytes 3538948
  294.4 38.8 %collective-permute-start.2 = (bf16[2,96,3072]{2,1,0:T(8,128)(2,1)S(1)}, bf16[2,96,3072]{2,1,0:T(8,128)(2,1)S(1)}, u32[]{:S(2)}, u32[]{:S(2)}) collective-permute-start(bf16[2,96,3072]{2,1,0:T(8,128)(2,1)S(1)} %bitcast.56), channel_id=1, source_target_pairs={{0,252},{4,0},{8,4},{12,8},{16,12},{20,16},{24,20},{28,24},{32,28}... | collective-permute-start | bytes 3538952 | tf_op jit(solution)/shard_map/ppermute | solution.py:37
Sparse Core Ops, SparseCore 0:
  9.8 180.0 all-gather.4
  191.7 95.5 all-gather.6
where the time goes:
time: 342 us; the launch traced here: 341 us
  waiting for transfers between devices  230 us (67%)
  starting transfers between devices  30.1 us (9%)
  matrix products  24.6 us (7%)
  local copies, waits for them, and re-layouts  17.9 us (5%)
  other arithmetic  16.4 us (5%)
  between operations  15.7 us (5%)
  blocking collectives  6.69 us (2%)
    all_gather x1, waiting for transfers between devices, per_device(): lax.all_gather(qkv_weight, 'mp', axis=0, tiled=True)  172 us
    all_gather x1, waiting for transfers between devices, per_device(): lax.all_gather(out_weight, 'mp', axis=0, tiled=True)  42.7 us
    ppermute x1, starting transfers between devices, from_behind(): return lax.ppermute(value, axis, pairs)  25.1 us
    ppermute x1, waiting for transfers between devices, from_behind(): return lax.ppermute(value, axis, pairs)  13.7 us
    dot_general x1, matrix products, per_device(): jnp.dot(picked, lax.all_gather(qkv_weight, 'mp', axis=0, tiled=True), pre...  12.2 us
    dot_general x1, matrix products, per_device(): jnp.dot(picked, lax.all_gather(out_weight, 'mp', axis=0, tiled=True), pre...  7.11 us
  transfers between devices with their start and end apart: 5, of which 3 were waited for; matrix products, arithmetic and copies ran while one was open for 14% of the time, Pallas kernels for 0%

commit v1 on v0

v1 whole, which is shorter than its diff:
```python
import functools
import math

import jax
import jax.numpy as jnp
from jax import lax
from jax.experimental import pallas as pl
from jax.experimental.pallas import tpu as pltpu
from jax.sharding import PartitionSpec as P

D = 3072
HEADS = 12
HEAD = 128
FREQ = 256
NOISE_LEVELS = 50
REACH_LIMIT = 2
SPATIAL = 96
FRAMES = 512
INNER = HEADS * HEAD
ROWS = 2 * SPATIAL
CHIP = 2 * ROWS
HALF = INNER // 2
PAIR = 2 * HEAD
WINDOW = (2 * REACH_LIMIT + 1) * SPATIAL
ROUNDS = 3
NY, NZ = 4, 8
MESH = pl.DeviceIdType.MESH
F32 = jnp.float32
BF16 = jnp.bfloat16

flow_shift = 7.0


def flow_sigma(position):
    return flow_shift * position / (1.0 + (flow_shift - 1.0) * position)


def level_terms(level_value):
    upper = (level_value + 1.0) / NOISE_LEVELS
    lower = level_value / NOISE_LEVELS
    sigma_now = flow_sigma(upper)
    step_size = sigma_now - flow_sigma(lower)
    half_count = FREQ // 2
    index_row = jnp.arange(half_count).astype(F32)
    frequency = jnp.exp(-math.log(10000.0) * index_row / half_count)
    angles = 1000.0 * sigma_now[:, None] * frequency[None, :]
    embedded = jnp.concatenate([jnp.cos(angles), jnp.sin(angles)], axis=-1)
    return (jax.nn.silu(embedded).astype(BF16), step_size)


HOPS = {
    ("z", "a", 1): 4, ("z", "a", -1): 3, ("z", "b", 1): 3, ("z", "b", -1): 4,
    ("y", "a", 1): 2, ("y", "a", -1): 1, ("y", "b", 1): 1, ("y", "b", -1): 2,
}


def kernel(
    x_hbm, w_hbm, wo_hbm, modpart, step, bias, qgain, kgain,
    vel_hbm, next_hbm,
    weights, out_weights, hidden, own_x, other_x, mod, shift, scale, gate,
    queries, keys, values, mixed, vel, stepped, send_sem, recv_sem, local_sem, mod_sem,
):
    f = lax.axis_index("frame")
    m = lax.axis_index("mp")
    xl = f % 2
    z = (f // 2) % NZ
    y = f // (2 * NZ)
    xh = m // 2
    c = m % 2

    def frame_of(yy, zz, ll):
        return (yy * NZ + zz) * 2 + ll

    twin = (f, xh * 2 + 1 - c)
    inner = (frame_of(y, z, 1 - xl), m)
    cross = [(frame_of(y, z, 1 - xl), (1 - xh) * 2 + core) for core in range(2)]
    ring = {
        ("z", 1): (frame_of(y, (z + 1) % NZ, xl), m),
        ("z", -1): (frame_of(y, (z + NZ - 1) % NZ, xl), m),
        ("y", 1): (frame_of((y + 1) % NY, z, xl), m),
        ("y", -1): (frame_of((y + NY - 1) % NY, z, xl), m),
    }
    group = [(f, (m + i) % 4) for i in range(1, 4)]
    count = 64
    before = [((f + count - 1) % count, xh * 2 + core) for core in range(2)]
    after = [((f + 1) % count, xh * 2 + core) for core in range(2)]
    chip_before = (f + count - 1 + xh) % count
    chip_after = (f + xh) % count
    halo = [(chip, (1 - xh) * 2 + core) for chip in (chip_before, chip_after) for core in range(2)]

    started = []
    numbers = {}

    def number(key):
        return numbers.setdefault(key, len(numbers))

    def remote(src, dst, key, device, keep=True):
        copy = pltpu.make_async_remote_copy(
            src_ref=src, dst_ref=dst, send_sem=send_sem.at[len(started) if keep else 0],
            recv_sem=recv_sem.at[key if not isinstance(key, tuple) else number(key)],
            device_id=device, device_id_type=MESH,
        )
        return copy

    def send(src, dst, key, device):
        copy = remote(src, dst, key, device)
        started.append(copy)
        copy.start()

    def received(dst, key):
        remote(dst, dst, key, twin, keep=False).wait_recv()

    locals_started = {}

    def load(src, dst, key, place):
        copy = pltpu.make_async_copy(src, dst, local_sem.at[place])
        copy.start()
        locals_started.setdefault(key, []).append(copy)

    load(x_hbm, own_x, "x", 0)
    for r in range(ROUNDS):
        for part in range(3):
            load(
                w_hbm.at[:, pl.ds(pl.multiple_of(part * INNER + c * HALF + r * PAIR, PAIR), PAIR)],
                weights.at[r, pl.ds(pl.multiple_of(m * 768, 768), 768), pl.ds(part * PAIR, PAIR)],
                r, 1 + r * 3 + part,
            )
    load(
        wo_hbm.at[:, pl.ds(pl.multiple_of(c * INNER, INNER), INNER)],
        out_weights.at[pl.ds(pl.multiple_of(m * 384, 384), 384)],
        ROUNDS, 1 + ROUNDS * 3,
    )
    mod[m] = modpart[...]

    barrier = pltpu.get_barrier_semaphore()
    greeted = [twin, inner, *cross, *ring.values(), *group[1:2], *before, *after, *halo]
    for device in greeted + [group[0], group[2]]:
        pl.semaphore_signal(barrier, inc=1, device_id=device, device_id_type=MESH)
    pl.semaphore_wait(barrier, len(greeted) + 2)

    buffers = [weights.at[r] for r in range(ROUNDS)] + [out_weights]
    shard = [768] * ROUNDS + [384]
    size = {"z": [48] * ROUNDS + [16], "y": [96] * ROUNDS + [64]}
    base = {"z": [0] * 4, "y": [384] * ROUNDS + [128]}
    own = {"z": z, "y": y}
    length = {"z": NZ, "y": NY}
    missing = (1 - xh) * 2
    shard_of = {"a": missing + xl, "b": missing + 1 - xl}

    def piece(axis, owner_shard, j, r):
        rows = size[axis][r]
        start = owner_shard * shard[r] + base[axis][r] + j * rows
        return buffers[r].at[pl.ds(pl.multiple_of(start, 16), rows)]

    fetched = []

    def fetch(r):
        first = len(started)

        @pl.when(c == 1 - xl)
        def _():
            for axis in ("z", "y"):
                rows = size[axis][r]
                here = pl.ds(pl.multiple_of(base[axis][r] + own[axis] * rows, 16), rows)
                there = pl.ds(
                    pl.multiple_of(m * shard[r] + base[axis][r] + own[axis] * rows, 16), rows
                )
                for core in range(2):
                    if r < ROUNDS:
                        for part in range(3):
                            send(
                                w_hbm.at[here, pl.ds(part * INNER + core * HALF + r * PAIR, PAIR)],
                                weights.at[r, there, pl.ds(part * PAIR, PAIR)],
                                ("fetch", axis, r), cross[core],
                            )
                    else:
                        send(
                            wo_hbm.at[here, pl.ds(core * INNER, INNER)],
                            out_weights.at[there],
                            ("fetch", axis, r), cross[core],
                        )

        for i in range(first, len(started)):
            rows = size["z" if i - first < (len(started) - first) // 2 else "y"][r]
            columns = pl.ds(0, PAIR if r < ROUNDS else INNER)
            source = (w_hbm if r < ROUNDS else wo_hbm).at[pl.ds(0, rows), columns]
            started[i] = None
            fetched.append((source, buffers[r].at[pl.ds(0, rows), columns], i))

    def exchange(r):
        if r < ROUNDS:
            for part in range(3):
                send(
                    w_hbm.at[:, pl.ds(pl.multiple_of(part * INNER + (1 - c) * HALF + r * PAIR, PAIR), PAIR)],
                    weights.at[r, pl.ds(pl.multiple_of(m * 768, 768), 768), pl.ds(part * PAIR, PAIR)],
                    ("twin", r), twin,
                )
        else:
            send(
                wo_hbm.at[:, pl.ds(pl.multiple_of((1 - c) * INNER, INNER), INNER)],
                out_weights.at[pl.ds(pl.multiple_of(m * 384, 384), 384)],
                ("twin", r), twin,
            )

    def ring_send(axis, way, half, k, r):
        if k >= HOPS[axis, half, way]:
            return
        j = (own[axis] - way * k + length[axis]) % length[axis]
        region = piece(axis, shard_of[half], j, r)
        send(region, region, (axis, way, half, k + 1, r), ring[axis, way])

    def ring_step(axis, half, k, r):
        for way in (1, -1):
            if k <= HOPS[axis, half, way]:
                j = (own[axis] - way * k + length[axis]) % length[axis]
                received(piece(axis, shard_of[half], j, r), (axis, way, half, k, r))
                ring_send(axis, way, half, k, r)

    def event(r, k):
        if k == 1:
            for axis in ("z", "y"):
                region = piece(axis, shard_of["a"], own[axis], r)
                received(region, ("fetch", axis, r))
                send(region, region, ("swap", axis, r), inner)
                for way in (1, -1):
                    ring_send(axis, way, "a", 0, r)
        elif k == 2:
            for axis in ("z", "y"):
                received(piece(axis, shard_of["b"], own[axis], r), ("swap", axis, r))
                for way in (1, -1):
                    ring_send(axis, way, "b", 0, r)
        else:
            steps = {
                3: [("z", "a", 1)], 4: [("z", "b", 1)], 5: [("z", "a", 2), ("y", "a", 1)],
                6: [("z", "b", 2)], 7: [("z", "a", 3), ("y", "b", 1)], 8: [("z", "b", 3)],
                9: [("z", "a", 4), ("z", "b", 4), ("y", "a", 2), ("y", "b", 2)],
            }[k]
            for axis, half, hop in steps:
                ring_step(axis, half, hop, r)

    def complete(r):
        for copy in locals_started.pop(r):
            copy.wait()
        rows = shard[r]
        start = (xh * 2 + 1 - c) * rows
        received(buffers[r].at[pl.ds(pl.multiple_of(start, rows), rows)], ("twin", r))

    for device in group:
        send(modpart, mod.at[m], mod_sem_key + m, device)
    fetch(0)
    exchange(0)
    send(
        x_hbm.at[:, pl.ds(pl.multiple_of((1 - c) * INNER, INNER), INNER)], other_x, ("x",), twin
    )
    for i in range(1, 4):
        source = (m + i) % 4
        received(mod.at[source], mod_sem_key + source)
    shift[:, :2304] = mod[0]
    shift[:, 2304:] = mod[1, :, :768]
    scale[:, :1536] = 1.0 + mod[1, :, 768:]
    scale[:, 1536:] = 1.0 + mod[2, :, :1536]
    gate[:, :768] = mod[2, :, 1536:]
    gate[:, 768:] = mod[3]
    for copy in locals_started.pop("x"):
        copy.wait()

    own_rows = pl.multiple_of(c * ROWS, ROWS)

    @pl.loop(0, ROWS // 16)
    def _(i):
        rows = own_x[pl.ds(pl.multiple_of(i * 16, 16), 16), :].astype(F32)
        center = jnp.mean(rows, axis=-1, keepdims=True)
        rows = rows - center
        spread = jnp.mean(rows * rows, axis=-1, keepdims=True)
        out = rows * lax.rsqrt(spread + 1e-06) * scale[...] + shift[...]
        hidden[pl.ds(pl.multiple_of(own_rows + i * 16, 16), 16), :] = out.astype(BF16)

    mine = hidden.at[pl.ds(own_rows, ROWS)]
    send(mine, mine, ("hidden",), twin)
    halo_chip = jnp.where(c == 1, chip_after, chip_before)
    halo_base = jnp.where(c == 1, CHIP, CHIP + ROWS)
    for core in range(2):
        send(
            hidden.at[pl.ds(pl.multiple_of(own_rows + core * SPATIAL, 16), SPATIAL)],
            hidden.at[pl.ds(pl.multiple_of(halo_base + core * SPATIAL, 16), SPATIAL)],
            halo_key + 1 - c, (halo_chip, (1 - xh) * 2 + core),
        )

    def halo_forward():
        for side in range(2):
            region = hidden.at[
                pl.ds(pl.multiple_of(CHIP + side * ROWS + c * SPATIAL, 16), SPATIAL)
            ]
            received(region, halo_key + side)
            send(region, region, ("forward", side), twin)

    def halo_arrived():
        for side in range(2):
            region = hidden.at[
                pl.ds(pl.multiple_of(CHIP + side * ROWS + (1 - c) * SPATIAL, 16), SPATIAL)
            ]
            received(region, ("forward", side))

    def product(lo, r, part):
        return jnp.dot(
            hidden[lo : lo + CHIP, :], weights[r, :, part * PAIR : (part + 1) * PAIR],
            preferred_element_type=F32,
        )

    def normed(tile, gain):
        return tile * lax.rsqrt(jnp.mean(tile * tile, axis=-1, keepdims=True) + 1e-06) * gain

    def project(r, part, own_part):
        tile = product(0 if own_part else CHIP, r, part)
        for h in range(2):
            columns = slice(h * HEAD, (h + 1) * HEAD)
            head = tile[:, columns]
            if part == 0:
                head = normed(head, qgain[...])
            elif part == 1:
                head = normed(head, kgain[...])
            head = head.astype(BF16)
            if part == 0:
                queries[r, :, columns] = head
            else:
                target = keys if part == 1 else values
                if own_part:
                    target[r, ROWS : ROWS + CHIP, columns] = head
                else:
                    target[r, 0:ROWS, columns] = head[:ROWS]
                    target[r, ROWS + CHIP :, columns] = head[ROWS:]

    def attend(r):
        @pl.loop(0, 4)
        def _(i):
            q_rows = pl.ds(pl.multiple_of(i * SPATIAL, 16), SPATIAL)
            k_rows = pl.ds(pl.multiple_of(i * SPATIAL, 16), WINDOW)
            for h in range(2):
                columns = slice(h * HEAD, (h + 1) * HEAD)
                scores = lax.dot_general(
                    queries[r, q_rows, columns], keys[r, k_rows, columns],
                    (((1,), (1,)), ((), ())), preferred_element_type=F32,
                ) + bias[i]
                peak = jnp.max(scores, axis=-1, keepdims=True)
                raised = jnp.exp(scores - peak)
                total = jnp.sum(raised, axis=-1, keepdims=True)
                out = jnp.dot(
                    raised.astype(BF16), values[r, k_rows, columns], preferred_element_type=F32
                )
                place = pl.multiple_of(c * HALF + r * PAIR + h * HEAD, HEAD)
                mixed[q_rows, pl.ds(place, HEAD)] = (out / total).astype(BF16)

        region = mixed.at[:, pl.ds(pl.multiple_of(c * HALF + r * PAIR, PAIR), PAIR)]
        send(region, region, ("mixed", r), twin)

    work = {
        9: [lambda: complete(0), lambda: project(0, 0, True)],
        10: [lambda: project(0, 1, True)],
        11: [lambda: project(0, 2, True)],
        15: [lambda: complete(1), lambda: project(1, 0, True)],
        16: [lambda: project(1, 1, True)],
        17: [halo_forward, lambda: project(1, 2, True)],
        18: [halo_arrived, lambda: project(0, 1, False)],
        19: [lambda: project(0, 2, False), lambda: attend(0)],
        20: [lambda: project(1, 1, False), lambda: project(1, 2, False)],
        21: [lambda: attend(1)],
        22: [lambda: complete(2), lambda: project(2, 0, True)],
        23: [lambda: project(2, 1, True), lambda: project(2, 1, False)],
        24: [lambda: project(2, 2, True), lambda: project(2, 2, False)],
        25: [lambda: attend(2)],
    }
    received_hidden = False
    for tick in range(1, 28):
        for r in range(4):
            k = tick - 6 * r
            if 1 <= k <= 9:
                event(r, k)
            if k == 2 and r < 3:
                fetch(r + 1)
                exchange(r + 1)
        if tick == 9 and not received_hidden:
            other = hidden.at[pl.ds(pl.multiple_of((1 - c) * ROWS, ROWS), ROWS)]
            received(other, ("hidden",))
            received_hidden = True
        for item in work.get(tick, []):
            item()
    complete(3)
    for r in range(ROUNDS):
        region = mixed.at[:, pl.ds(pl.multiple_of((1 - c) * HALF + r * PAIR, PAIR), PAIR)]
        received(region, ("mixed", r))
    received(other_x, ("x",))

    half_columns = pl.multiple_of(c * INNER, INNER)
    step_row = step[...]
    groups = 3
    wide = INNER // groups
    finals = []
    for g in range(groups):
        for t in range(2):
            lo = g * wide + t * PAIR
            attended = jnp.dot(
                mixed[...], out_weights[:, lo : lo + PAIR], preferred_element_type=F32
            )
            gate_row = gate[:, pl.ds(pl.multiple_of(half_columns + lo, PAIR), PAIR)]
            mine_x = own_x[:, pl.ds(pl.multiple_of(half_columns + lo, PAIR), PAIR)].astype(F32)
            twin_x = other_x[:, lo : lo + PAIR].astype(F32)
            for base_x, at in ((mine_x, own_rows), (twin_x, ROWS - own_rows)):
                at = pl.multiple_of(at, ROWS)
                stage = pl.ds(at, ROWS)
                vel[stage, lo : lo + PAIR] = base_x.astype(BF16)
            base_x = vel[:, lo : lo + PAIR].astype(F32)
            full = base_x + gate_row * attended
            vel[:, lo : lo + PAIR] = full.astype(BF16)
            stepped[:, lo : lo + PAIR] = (base_x - step_row * full).astype(BF16)
        columns = pl.ds(pl.multiple_of(half_columns + g * wide, wide), wide)
        stage_columns = pl.ds(g * wide, wide)
        for core in range(2):
            send(
                stepped.at[pl.ds(core * ROWS, ROWS), stage_columns],
                next_hbm.at[:, columns], next_key + 2 * g + c, before[core],
            )
        twin_rows = pl.ds(pl.multiple_of((1 - c) * ROWS, ROWS), ROWS)
        send(
            vel.at[twin_rows, stage_columns], vel_hbm.at[:, columns], ("velocity", g), twin
        )
        copy = pltpu.make_async_copy(
            vel.at[pl.ds(own_rows, ROWS), stage_columns], vel_hbm.at[:, columns],
            local_sem.at[11 + g],
        )
        copy.start()
        finals.append(copy)
    for g in range(groups):
        for core in range(2):
            received(next_hbm.at[:, pl.ds(core * INNER + g * wide, wide)], next_key + 2 * g + core)
        columns = pl.ds(pl.multiple_of((1 - c) * INNER + g * wide, wide), wide)
        received(vel_hbm.at[:, columns], ("velocity", g))
    for copy in finals:
        copy.wait()
    assert len(started) <= SENDS and len(numbers) <= mod_sem_key
    for copy in started:
        if copy is not None:
            copy.wait_send()

    @pl.when(c == 1 - xl)
    def _():
        for src, dst, i in fetched:
            pltpu.make_async_remote_copy(
                src_ref=src, dst_ref=dst, send_sem=send_sem.at[i], recv_sem=recv_sem.at[0],
                device_id=twin, device_id_type=MESH,
            ).wait_send()


mod_sem_key = 160
halo_key = 164
next_key = 166
SEMAPHORES = 172
SENDS = 256


def per_device(
    latents, levels, window_reach, query_gain, key_gain, qkv_weight, out_weight, mod_weight
):
    activity, step_size = level_terms(levels.astype(F32))
    own_part = jnp.dot(activity, mod_weight, preferred_element_type=F32)
    f = lax.axis_index("frame")
    first = f * 8 + (lax.axis_index("mp") // 2) * 4
    offset = jnp.arange(WINDOW, dtype=jnp.int32) // SPATIAL - REACH_LIMIT
    key_frame = first + jnp.arange(4, dtype=jnp.int32)[:, None] + offset[None, :]
    valid = (jnp.abs(offset)[None, :] <= window_reach[0]) & (key_frame >= 0) & (key_frame < FRAMES)
    bias = jnp.where(valid, 0.0, -1e30).astype(F32).reshape(4, 1, WINDOW)
    step_row = jnp.broadcast_to(step_size.reshape(1, 1), (1, PAIR))
    vmem = pl.BlockSpec(memory_space=pltpu.VMEM)
    hbm = pl.BlockSpec(memory_space=pl.ANY)
    shape = jax.ShapeDtypeStruct((ROWS, D), BF16)
    velocity, queue_next = pl.pallas_call(
        kernel,
        out_shape=(shape, shape),
        in_specs=[hbm, hbm, hbm, vmem, vmem, vmem, vmem, vmem],
        out_specs=(hbm, hbm),
        scratch_shapes=[
            pltpu.VMEM((ROUNDS, D, 3 * PAIR), BF16),
            pltpu.VMEM((INNER, INNER), BF16),
            pltpu.VMEM((2 * CHIP, D), BF16),
            pltpu.VMEM((ROWS, D), BF16),
            pltpu.VMEM((ROWS, INNER), BF16),
            pltpu.VMEM((4, 1, 2304), F32),
            pltpu.VMEM((1, D), F32),
            pltpu.VMEM((1, D), F32),
            pltpu.VMEM((1, D), F32),
            pltpu.VMEM((ROUNDS, CHIP, PAIR), BF16),
            pltpu.VMEM((ROUNDS, 2 * CHIP, PAIR), BF16),
            pltpu.VMEM((ROUNDS, 2 * CHIP, PAIR), BF16),
            pltpu.VMEM((CHIP, INNER), BF16),
            pltpu.VMEM((CHIP, INNER), BF16),
            pltpu.VMEM((CHIP, INNER), BF16),
            pltpu.SemaphoreType.DMA((SENDS,)),
            pltpu.SemaphoreType.DMA((SEMAPHORES,)),
            pltpu.SemaphoreType.DMA((16,)),
            pltpu.SemaphoreType.DMA((1,)),
        ],
        compiler_params=pltpu.CompilerParams(
            collective_id=0, has_side_effects=True, vmem_limit_bytes=56 * 2**20
        ),
    )(
        latents.reshape(ROWS, D), qkv_weight, out_weight, own_part, step_row, bias,
        (query_gain / math.sqrt(HEAD)).reshape(1, HEAD), key_gain.reshape(1, HEAD),
    )
    return (queue_next.reshape(2, SPATIAL, D), velocity.reshape(2, SPATIAL, D))


def solution(mesh):
    return jax.shard_map(
        per_device,
        mesh=mesh,
        in_specs=(
            P(("frame", "mp"), None, None),
            P("frame"),
            P("frame"),
            P(),
            P(),
            P("mp", None),
            P("mp", None),
            P(None, "mp"),
        ),
        out_specs=(P(("frame", "mp"), None, None), P(("frame", "mp"), None, None)),
        check_vma=False,
    )
```

time: 342 us -> 148 us (0.43)
  the two profiles are of different devices: /device:TPU:0 before, /device:TPU:1 now
where the time goes in v1:
time: 148 us; the launch traced here: 146 us
  Pallas kernels  137 us (93%)
  local copies, waits for them, and re-layouts  4.07 us (3%)
  between operations  2.18 us (1%)
  other arithmetic  1.94 us (1%)
    pallas_call x1, Pallas kernels, per_device(): pl.pallas_call(kernel, out_shape=(shape, shape), in_specs=[hbm, hbm, hbm,...  137 us
    unnamed x6, local copies, waits for them, and re-layouts  3.48 us

profile of v1, /device:TPU:1, one launch (start us, length us, event | category | flops | bytes accessed | tf_op | source)
XLA Modules:
  0.0 146.1 jit_solution(5642470106724861451)
XLA Ops:
  0.6 0.0 copy-start
  2.2 1.2 multiply_bitcast_fusion.qgain
  3.3 0.6 broadcast_in_dim.21.step
  4.0 0.7 and_select_fusion.bias
  4.7 0.0 copy-done
  4.7 0.9 fusion.7.modpart
  5.6 137.0 %shard_map.95 = (bf16[192,3072]{1,0:T(8,128)(2,1)}, bf16[192,3072]{1,0:T(8,128)(2,1)}) custom-call(bf16[192,3072]{1,0:T(8,128)(2,1)} %bitcast.12, bf16[768,4608]{1,0:T(8,128)(2,1)} %w_hbm.1, bf16[384,3072]{1,0:T(8,128)(2,1)} %wo_hbm.1, f32[1,2304]{1,0:T(1,128)} %fusion.7.modpart, f32[1,256]{1,0:T(1,128)} %broadcast_in_dim.21.step, ...), custom_call_target="tpu_custom_call" | custom-call | tf_op jit(solution)/shard_map/pallas_call | solution.py:475
  142.6 0.0 copy-start.1
  142.6 2.5 %copy.14 = bf16[2,96,3072]{2,1,0:T(8,128)(2,1)} copy(bf16[2,96,3072]{2,1,0:T(8,128)(2,1)} %bitcast.14) | data formatting | bytes 2359296
  145.0 0.0 copy-done.1
  145.0 1.0 copy.15
  (6 shorter events, 0.1 us)
Async XLA Ops:
  0.6 4.1 %copy-start = (bf16[256,2304]{1,0:T(8,128)(2,1)S(1)}, bf16[256,2304]{1,0:T(8,128)(2,1)}, u32[]{:S(2)}) copy-start(bf16[256,2304]{1,0:T(8,128)(2,1)} %param.15) | copy-start | bytes 3538948
  142.6 2.5 %copy-start.1 = (bf16[192,3072]{1,0:T(8,128)(2,1)S(1)}, bf16[192,3072]{1,0:T(8,128)(2,1)}, u32[]{:S(2)}) copy-start(bf16[192,3072]{1,0:T(8,128)(2,1)} %get-tuple-element.5) | copy-start | bytes 3538948

commit v2 on v1

v2 whole, which is shorter than its diff:
```python
import heapq
import math

import jax
import jax.numpy as jnp
from jax import lax
from jax.experimental import pallas as pl
from jax.experimental.pallas import tpu as pltpu
from jax.sharding import PartitionSpec as P

D = 3072
HEADS = 12
HEAD = 128
FREQ = 256
NOISE_LEVELS = 50
REACH_LIMIT = 2
SPATIAL = 96
FRAMES = 512
INNER = HEADS * HEAD
ROWS = 2 * SPATIAL
CHIP = 2 * ROWS
HALF = INNER // 2
PAIR = 2 * HEAD
WINDOW = (2 * REACH_LIMIT + 1) * SPATIAL
ROUNDS = 3
NY, NZ = 4, 8
MESH = pl.DeviceIdType.MESH
F32 = jnp.float32
BF16 = jnp.bfloat16

flow_shift = 7.0


def flow_sigma(position):
    return flow_shift * position / (1.0 + (flow_shift - 1.0) * position)


HOPS = {
    ("z", "a", 1): 4, ("z", "a", -1): 3, ("z", "b", 1): 3, ("z", "b", -1): 4,
    ("y", "a", 1): 2, ("y", "a", -1): 1, ("y", "b", 1): 1, ("y", "b", -1): 2,
}
SHARD = [768] * ROUNDS + [384] * 2
PIECE = {"z": [48] * ROUNDS + [0] * 2, "y": [96] * ROUNDS + [96] * 2}
BASE = {"z": [0] * 5, "y": [384] * ROUNDS + [0] * 2}
AXES = [[axis for axis in "zy" if PIECE[axis][r]] for r in range(5)]
WIDE = 3 * PAIR


def plan():
    rate, latency, backlog, halo_time = 46500.0, 2.2, 2.2, 25.0
    busy, ready, arrivals, actions, work, waiting = {}, {}, [], [], [], []

    def cost(axis, r):
        return PIECE[axis][r] * WIDE * 2 / rate

    def transmit(link, time, length, what):
        busy[link] = max(busy.get(link, 0.0), time) + length
        heapq.heappush(arrivals, (busy[link] + latency, len(actions), len(arrivals), what))

    def offer(axis, way, half, k, r):
        rest = HOPS[axis, half, way] - k
        if rest > 0:
            item = (r, -rest, len(actions), ("ring", axis, way, half, k, r))
            ready.setdefault((axis, way), []).append(item)

    left = [0] * 5
    for r in range(5):
        for axis in AXES[r]:
            left[r] += 2 + sum(hops for key, hops in HOPS.items() if key[0] == axis)
            transmit("cross", 0.0, cost(axis, r), ("fetch", axis, r))
    swaps = sum(len(axes) for axes in AXES)
    now = 6.0
    transmit("cross", now, halo_time, ("halo",))
    halo = False

    def halo_work(r):
        return [("project", r, 1, False), ("project", r, 2, False), ("attend", r)]

    while True:
        if arrivals and arrivals[0][0] <= now:
            what = heapq.heappop(arrivals)[-1]
            actions.append(("wait", *what))
            now += 0.05
            if what[0] == "halo":
                halo = True
                work.append(("halo",))
                for r in waiting:
                    work.extend(halo_work(r))
                continue
            r = what[-1]
            left[r] -= 1
            if what[0] == "fetch":
                ready.setdefault("inner", []).append((r, 0, len(actions), ("swap", what[1], r)))
            if what[0] == "ring":
                offer(*what[1:])
            else:
                for way in (1, -1):
                    offer(what[1], way, "a" if what[0] == "fetch" else "b", 0, r)
            if left[r] == 0 and r < ROUNDS:
                work.append(("complete", r))
                work.extend(("project", r, part, True) for part in range(3))
                if halo:
                    work.extend(halo_work(r))
                else:
                    waiting.append(r)
            continue
        sent = False
        for link, queue in ready.items():
            if queue and busy.get(link, 0.0) - now < backlog:
                queue.sort()
                item = queue.pop(0)[-1]
                actions.append(("send", *item))
                now += 0.05
                sent = True
                if item[0] == "swap":
                    transmit(link, now, cost(item[1], item[2]), item)
                    swaps -= 1
                    if swaps == 0:
                        actions.append(("next",))
                else:
                    kind, axis, way, half, k, r = item
                    transmit(link, now, cost(axis, r), (kind, axis, way, half, k + 1, r))
        if sent:
            continue
        if work:
            item = work.pop(0)
            actions.append(item)
            now += {"project": 0.75, "attend": 2.0}.get(item[0], 0.2)
            continue
        later = [arrivals[0][0]] if arrivals else []
        later += [busy[link] - backlog + 0.01 for link, queue in ready.items() if queue]
        if not later:
            return actions
        now = max(now, min(later))


def kernel(
    x_hbm, w_hbm, wo_hbm, mw_hbm, levels, reach, qgain, kgain,
    vel_hbm, next_hbm,
    weights, out_weights, hidden, own_x, half_x, next_x, mod_weights, part_mod, mod, shift, scale,
    gate, next_gate, queries, keys, values, mixed, next_mixed, vel, stepped,
    send_sem, recv_sem, local_sem,
):
    f = lax.axis_index("frame")
    m = lax.axis_index("mp")
    xl = f % 2
    z = (f // 2) % NZ
    y = f // (2 * NZ)
    xh = m // 2
    c = m % 2

    def frame_of(yy, zz, ll):
        return (yy * NZ + zz) * 2 + ll

    twin = (f, xh * 2 + 1 - c)
    inner = (frame_of(y, z, 1 - xl), m)
    cross = [(frame_of(y, z, 1 - xl), (1 - xh) * 2 + core) for core in range(2)]
    ring = {
        ("z", 1): (frame_of(y, (z + 1) % NZ, xl), m),
        ("z", -1): (frame_of(y, (z + NZ - 1) % NZ, xl), m),
        ("y", 1): (frame_of((y + 1) % NY, z, xl), m),
        ("y", -1): (frame_of((y + NY - 1) % NY, z, xl), m),
    }
    group = [(f, (m + i) % 4) for i in range(1, 4)]
    count = 64
    before = [((f + count - 1) % count, xh * 2 + core) for core in range(2)]
    after = [((f + 1) % count, xh * 2 + core) for core in range(2)]
    chip_before = (f + count - 1 + xh) % count
    chip_after = (f + xh) % count
    halo = [(chip, (1 - xh) * 2 + core) for chip in (chip_before, chip_after) for core in range(2)]

    started = []
    numbers = {}

    def number(key):
        return numbers.setdefault(key, len(numbers))

    def remote(src, dst, key, device, keep=True):
        copy = pltpu.make_async_remote_copy(
            src_ref=src, dst_ref=dst, send_sem=send_sem.at[len(started) if keep else 0],
            recv_sem=recv_sem.at[key if not isinstance(key, tuple) else number(key)],
            device_id=device, device_id_type=MESH,
        )
        return copy

    def send(src, dst, key, device):
        copy = remote(src, dst, key, device)
        started.append(copy)
        copy.start()

    def received(dst, key):
        remote(dst, dst, key, twin, keep=False).wait_recv()

    locals_started = {}

    def load(src, dst, key, place):
        copy = pltpu.make_async_copy(src, dst, local_sem.at[place])
        copy.start()
        locals_started.setdefault(key, []).append(copy)

    barrier = pltpu.get_barrier_semaphore()
    greeted = [twin, inner, *cross, *ring.values(), *group, *before, *after, *halo]
    for device in greeted:
        pl.semaphore_signal(barrier, inc=1, device_id=device, device_id_type=MESH)

    half_columns = pl.multiple_of(c * INNER, INNER)
    other_columns = pl.multiple_of((1 - c) * INNER, INNER)
    own_rows = pl.multiple_of(c * ROWS, ROWS)
    buffers = [weights.at[r] for r in range(ROUNDS)] + [out_weights.at[r] for r in range(2)]
    load(mw_hbm, mod_weights, "mod", 0)
    load(x_hbm, own_x, "x", 1)
    load(x_hbm.at[:, pl.ds(half_columns, INNER)], half_x.at[pl.ds(own_rows, ROWS)], "half", 2)

    def slabs(r, core):
        if r < ROUNDS:
            for part in range(3):
                start = part * INNER + core * HALF + r * PAIR
                yield pl.ds(pl.multiple_of(start, PAIR), PAIR), pl.ds(part * PAIR, PAIR)
        else:
            start = core * INNER + (r - ROUNDS) * WIDE
            yield pl.ds(pl.multiple_of(start, WIDE), WIDE), pl.ds(0, WIDE)

    def source(r):
        return w_hbm if r < ROUNDS else wo_hbm

    def shard_rows(r, owner):
        return pl.ds(pl.multiple_of(owner * SHARD[r], SHARD[r]), SHARD[r])

    for r in range(5):
        for i, (here, there) in enumerate(slabs(r, c)):
            load(source(r).at[:, here], buffers[r].at[shard_rows(r, m), there], r, 3 + 3 * r + i)

    level = jnp.full((16, HEAD), levels[0], jnp.int32).astype(F32)
    sigma_now = flow_sigma((level + 1.0) / NOISE_LEVELS)
    step_size = sigma_now - flow_sigma(level / NOISE_LEVELS)
    index_row = lax.broadcasted_iota(jnp.int32, (16, HEAD), 1).astype(F32)
    angles = 1000.0 * sigma_now * jnp.exp(-math.log(10000.0) * index_row / HEAD)
    waves = [jax.nn.silu(wave(angles)).astype(BF16) for wave in (jnp.cos, jnp.sin)]
    for copy in locals_started.pop("mod"):
        copy.wait()
    columns_mod = jnp.dot(waves[0], mod_weights[:HEAD], preferred_element_type=F32)
    columns_mod += jnp.dot(waves[1], mod_weights[HEAD:], preferred_element_type=F32)
    part_mod[...] = columns_mod[:1]
    mod[m] = columns_mod[:1]
    pl.semaphore_wait(barrier, len(greeted))

    own = {"z": z, "y": y}
    length = {"z": NZ, "y": NY}
    missing = (1 - xh) * 2
    shard_of = {"a": missing + xl, "b": missing + 1 - xl}

    def piece(axis, owner, j, r):
        rows = PIECE[axis][r]
        start = owner * SHARD[r] + BASE[axis][r] + j * rows
        return buffers[r].at[pl.ds(pl.multiple_of(start, 16), rows)]

    fetched = []

    def fetch(r):
        first = len(started)

        @pl.when(c == 1 - xl)
        def _():
            for axis in AXES[r]:
                rows = PIECE[axis][r]
                start = BASE[axis][r] + own[axis] * rows
                rows_here = pl.ds(pl.multiple_of(start, 16), rows)
                rows_there = pl.ds(pl.multiple_of(m * SHARD[r] + start, 16), rows)
                for core in range(2):
                    for here, there in slabs(r, core):
                        send(
                            source(r).at[rows_here, here], buffers[r].at[rows_there, there],
                            ("fetch", axis, r), cross[core],
                        )

        each = (len(started) - first) // len(AXES[r])
        for i in range(first, len(started)):
            rows = PIECE[AXES[r][(i - first) // each]][r]
            region = buffers[r].at[pl.ds(0, rows), pl.ds(0, PAIR if r < ROUNDS else WIDE)]
            started[i] = None
            fetched.append((region, i))

    def exchange(r):
        for here, there in slabs(r, 1 - c):
            send(
                source(r).at[:, here], buffers[r].at[shard_rows(r, m), there], ("twin", r), twin
            )

    def ring_send(axis, way, half, k, r):
        if k >= HOPS[axis, half, way]:
            return
        j = (own[axis] - way * k + length[axis]) % length[axis]
        region = piece(axis, shard_of[half], j, r)
        send(region, region, (axis, way, half, k + 1, r), ring[axis, way])

    def arrived(axis, way, half, k, r):
        j = (own[axis] - way * k + length[axis]) % length[axis]
        received(piece(axis, shard_of[half], j, r), (axis, way, half, k, r))

    def complete(r):
        for copy in locals_started.pop(r):
            copy.wait()
        received(buffers[r].at[shard_rows(r, xh * 2 + 1 - c)], ("twin", r))

    for device in group:
        send(part_mod, mod.at[m], mod_sem_key + m, device)
    fetch(0)
    fetch(1)
    send(
        x_hbm.at[:, pl.ds(other_columns, INNER)], half_x.at[pl.ds(own_rows, ROWS)], ("x",), twin
    )
    for r in range(5):
        exchange(r)
    for r in range(2, 5):
        fetch(r)
    for i in range(1, 4):
        owner = (m + i) % 4
        received(mod.at[owner], mod_sem_key + owner)
    shift[:, :2304] = mod[0]
    shift[:, 2304:] = mod[1, :, :768]
    scale[:, :1536] = 1.0 + mod[1, :, 768:]
    scale[:, 1536:] = 1.0 + mod[2, :, :1536]
    gate[:, :768] = mod[2, :, 1536:]
    gate[:, 768:D] = mod[3]
    gate[:, D:] = step_size[:1]
    slot_before = (f + count - 1) % count
    send(gate, next_gate, ("gate",), (slot_before, m))
    for copy in locals_started.pop("x"):
        copy.wait()

    @pl.loop(0, ROWS // 16)
    def _(i):
        rows = own_x[pl.ds(pl.multiple_of(i * 16, 16), 16), :].astype(F32)
        center = jnp.mean(rows, axis=-1, keepdims=True)
        rows = rows - center
        spread = jnp.mean(rows * rows, axis=-1, keepdims=True)
        out = rows * lax.rsqrt(spread + 1e-06) * scale[...] + shift[...]
        hidden[pl.ds(pl.multiple_of(own_rows + i * 16, 16), 16), :] = out.astype(BF16)

    mine = hidden.at[pl.ds(own_rows, ROWS)]
    send(mine, mine, ("hidden",), twin)
    halo_chip = jnp.where(c == 1, chip_after, chip_before)
    halo_base = jnp.where(c == 1, CHIP, CHIP + ROWS)
    for core in range(2):
        send(
            hidden.at[pl.ds(pl.multiple_of(own_rows + core * SPATIAL, 16), SPATIAL)],
            hidden.at[pl.ds(pl.multiple_of(halo_base + core * SPATIAL, 16), SPATIAL)],
            halo_key + 1 - c, (halo_chip, (1 - xh) * 2 + core),
        )

    def halo_forward():
        for side in range(2):
            region = hidden.at[
                pl.ds(pl.multiple_of(CHIP + side * ROWS + c * SPATIAL, 16), SPATIAL)
            ]
            received(region, halo_key + side)
            send(region, region, ("forward", side), twin)

    def halo_arrived():
        for side in range(2):
            region = hidden.at[
                pl.ds(pl.multiple_of(CHIP + side * ROWS + (1 - c) * SPATIAL, 16), SPATIAL)
            ]
            received(region, ("forward", side))

    def product(lo, r, part):
        return jnp.dot(
            hidden[lo : lo + CHIP, :], weights[r, :, part * PAIR : (part + 1) * PAIR],
            preferred_element_type=F32,
        )

    def normed(tile, gain):
        return tile * lax.rsqrt(jnp.mean(tile * tile, axis=-1, keepdims=True) + 1e-06) * gain

    def project(r, part, own_part):
        tile = product(0 if own_part else CHIP, r, part)
        for h in range(2):
            columns = slice(h * HEAD, (h + 1) * HEAD)
            head = tile[:, columns]
            if part == 0:
                head = normed(head, qgain[...] * (1.0 / math.sqrt(HEAD)))
            elif part == 1:
                head = normed(head, kgain[...])
            head = head.astype(BF16)
            if part == 0:
                queries[r, :, columns] = head
            else:
                target = keys if part == 1 else values
                if own_part:
                    target[r, ROWS : ROWS + CHIP, columns] = head
                else:
                    target[r, 0:ROWS, columns] = head[:ROWS]
                    target[r, ROWS + CHIP :, columns] = head[ROWS:]

    lane = lax.broadcasted_iota(jnp.int32, (1, WINDOW), 1)
    offset = sum((lane >= k * SPATIAL).astype(jnp.int32) for k in range(1, 5)) - REACH_LIMIT

    def attend(r):
        @pl.loop(0, 4)
        def _(i):
            q_rows = pl.ds(pl.multiple_of(i * SPATIAL, 16), SPATIAL)
            k_rows = pl.ds(pl.multiple_of(i * SPATIAL, 16), WINDOW)
            key_frame = f * 8 + xh * 4 + i + offset
            valid = (jnp.abs(offset) <= reach[0]) & (key_frame >= 0) & (key_frame < FRAMES)
            bias = jnp.where(valid, 0.0, -1e30)
            for h in range(2):
                columns = slice(h * HEAD, (h + 1) * HEAD)
                scores = lax.dot_general(
                    queries[r, q_rows, columns], keys[r, k_rows, columns],
                    (((1,), (1,)), ((), ())), preferred_element_type=F32,
                ) + bias
                peak = jnp.max(scores, axis=-1, keepdims=True)
                raised = jnp.exp(scores - peak)
                total = jnp.sum(raised, axis=-1, keepdims=True)
                out = jnp.dot(
                    raised.astype(BF16), values[r, k_rows, columns], preferred_element_type=F32
                )
                place = pl.multiple_of(c * HALF + r * PAIR + h * HEAD, HEAD)
                mixed[q_rows, pl.ds(place, HEAD)] = (out / total).astype(BF16)

        columns = pl.ds(pl.multiple_of(c * HALF + r * PAIR, PAIR), PAIR)
        send(mixed.at[:, columns], next_mixed.at[:, columns], ("next mixed", r), (slot_before, m))
        send(mixed.at[:, columns], mixed.at[:, columns], ("mixed", r), twin)

    def forward_mixed(r):
        region = next_mixed.at[:, pl.ds(pl.multiple_of(c * HALF + r * PAIR, PAIR), PAIR)]
        received(region, ("next mixed", r))
        send(region, region, ("forward mixed", r), twin)

    def all_mixed(buffer, name):
        for r in range(ROUNDS):
            columns = pl.ds(pl.multiple_of((1 - c) * HALF + r * PAIR, PAIR), PAIR)
            received(buffer.at[:, columns], (name, r))

    first = True
    for action in plan():
        kind, rest = action[0], action[1:]
        if kind == "wait":
            kind, rest = rest[0], rest[1:]
            if kind == "fetch":
                received(piece(rest[0], shard_of["a"], own[rest[0]], rest[1]), ("fetch", *rest))
            elif kind == "swap":
                received(piece(rest[0], shard_of["b"], own[rest[0]], rest[1]), ("swap", *rest))
            elif kind == "ring":
                arrived(*rest)
            else:
                halo_forward()
        elif kind == "send":
            kind, rest = rest[0], rest[1:]
            if kind == "swap":
                region = piece(rest[0], shard_of["a"], own[rest[0]], rest[1])
                send(region, region, ("swap", *rest), inner)
            else:
                ring_send(*rest)
        elif kind == "next":
            for core in range(2):
                send(
                    x_hbm.at[:, pl.ds(core * INNER, INNER)], next_x.at[pl.ds(own_rows, ROWS)],
                    next_x_key + c, before[core],
                )
        elif kind == "complete":
            complete(*rest)
            if first:
                other = hidden.at[pl.ds(pl.multiple_of((1 - c) * ROWS, ROWS), ROWS)]
                received(other, ("hidden",))
                first = False
        elif kind == "project":
            project(*rest)
        elif kind == "attend":
            attend(*rest)
        else:
            halo_arrived()

    finals = []

    def finish(buffer, base_rows, gates, out, out_hbm, next_slot):
        for h in range(2):
            for t in range(3):
                lo = h * WIDE + t * PAIR
                attended = jnp.dot(
                    buffer[...], out_weights[h, :, t * PAIR : (t + 1) * PAIR],
                    preferred_element_type=F32,
                )
                gate_row = gates[:, pl.ds(pl.multiple_of(half_columns + lo, PAIR), PAIR)]
                rows = base_rows[:, lo : lo + PAIR].astype(F32)
                full = rows + gate_row * attended
                if next_slot:
                    step = jnp.concatenate([gates[:, D:]] * 2, axis=1)
                    full = rows - step * full
                out[:, lo : lo + PAIR] = full.astype(BF16)
            columns = pl.ds(pl.multiple_of(half_columns + h * WIDE, WIDE), WIDE)
            stage = pl.ds(h * WIDE, WIDE)
            twin_rows = pl.ds(pl.multiple_of((1 - c) * ROWS, ROWS), ROWS)
            send(
                out.at[twin_rows, stage], out_hbm.at[:, columns], ("out", next_slot, h), twin
            )
            copy = pltpu.make_async_copy(
                out.at[pl.ds(own_rows, ROWS), stage], out_hbm.at[:, columns],
                local_sem.at[18 + len(finals)],
            )
            copy.start()
            finals.append(copy)

    forward_mixed(0)
    complete(3)
    complete(4)
    for copy in locals_started.pop("half"):
        copy.wait()
    received(half_x.at[pl.ds(pl.multiple_of((1 - c) * ROWS, ROWS), ROWS)], ("x",))
    all_mixed(mixed, "mixed")
    finish(mixed, half_x, gate, vel, vel_hbm, False)
    forward_mixed(1)
    forward_mixed(2)
    received(next_gate, ("gate",))
    for core in range(2):
        received(next_x.at[pl.ds(core * ROWS, ROWS)], next_x_key + core)
    all_mixed(next_mixed, "forward mixed")
    finish(next_mixed, next_x, next_gate, stepped, next_hbm, True)
    for h in range(2):
        columns = pl.ds(pl.multiple_of(other_columns + h * WIDE, WIDE), WIDE)
        received(vel_hbm.at[:, columns], ("out", False, h))
        received(next_hbm.at[:, columns], ("out", True, h))
    for copy in finals:
        copy.wait()
    assert len(started) <= SENDS and len(numbers) <= mod_sem_key
    for copy in started:
        if copy is not None:
            copy.wait_send()

    @pl.when(c == 1 - xl)
    def _():
        for region, i in fetched:
            pltpu.make_async_remote_copy(
                src_ref=region, dst_ref=region, send_sem=send_sem.at[i], recv_sem=recv_sem.at[0],
                device_id=twin, device_id_type=MESH,
            ).wait_send()


mod_sem_key = 160
halo_key = 164
next_x_key = 166
SEMAPHORES = 168
SENDS = 288


def per_device(
    latents, levels, window_reach, query_gain, key_gain, qkv_weight, out_weight, mod_weight
):
    vmem = pl.BlockSpec(memory_space=pltpu.VMEM)
    smem = pl.BlockSpec(memory_space=pltpu.SMEM)
    hbm = pl.BlockSpec(memory_space=pl.ANY)
    shape = jax.ShapeDtypeStruct((ROWS, D), BF16)
    velocity, queue_next = pl.pallas_call(
        kernel,
        out_shape=(shape, shape),
        in_specs=[hbm, hbm, hbm, hbm, smem, smem, vmem, vmem],
        out_specs=(hbm, hbm),
        scratch_shapes=[
            pltpu.VMEM((ROUNDS, D, WIDE), BF16),
            pltpu.VMEM((2, INNER, WIDE), BF16),
            pltpu.VMEM((2 * CHIP, D), BF16),
            pltpu.VMEM((ROWS, D), BF16),
            pltpu.VMEM((CHIP, INNER), BF16),
            pltpu.VMEM((CHIP, INNER), BF16),
            pltpu.VMEM((FREQ, 2304), BF16),
            pltpu.VMEM((1, 2304), F32),
            pltpu.VMEM((4, 1, 2304), F32),
            pltpu.VMEM((1, D), F32),
            pltpu.VMEM((1, D), F32),
            pltpu.VMEM((1, D + HEAD), F32),
            pltpu.VMEM((1, D + HEAD), F32),
            pltpu.VMEM((ROUNDS, CHIP, PAIR), BF16),
            pltpu.VMEM((ROUNDS, 2 * CHIP, PAIR), BF16),
            pltpu.VMEM((ROUNDS, 2 * CHIP, PAIR), BF16),
            pltpu.VMEM((CHIP, INNER), BF16),
            pltpu.VMEM((CHIP, INNER), BF16),
            pltpu.VMEM((CHIP, INNER), BF16),
            pltpu.VMEM((CHIP, INNER), BF16),
            pltpu.SemaphoreType.DMA((SENDS,)),
            pltpu.SemaphoreType.DMA((SEMAPHORES,)),
            pltpu.SemaphoreType.DMA((24,)),
        ],
        compiler_params=pltpu.CompilerParams(
            collective_id=0, has_side_effects=True, vmem_limit_bytes=56 * 2**20
        ),
    )(
        latents.reshape(ROWS, D), qkv_weight, out_weight, mod_weight, levels, window_reach,
        query_gain.reshape(1, HEAD), key_gain.reshape(1, HEAD),
    )
    return (queue_next.reshape(2, SPATIAL, D), velocity.reshape(2, SPATIAL, D))


def solution(mesh):
    return jax.shard_map(
        per_device,
        mesh=mesh,
        in_specs=(
            P(("frame", "mp"), None, None),
            P("frame"),
            P("frame"),
            P(),
            P(),
            P("mp", None),
            P("mp", None),
            P(None, "mp"),
        ),
        out_specs=(P(("frame", "mp"), None, None), P(("frame", "mp"), None, None)),
        check_vma=False,
    )
```

time: 148 us -> 146 us (0.986); the launches traced: 146 us -> 146 us
  Pallas kernels: 137 us -> 141 us
  other arithmetic: 1.94 us -> 0 us
    pallas_call x1, Pallas kernels: 137 us -> 141 us  [per_device(): pl.pallas_call(kernel, out_shape=(shape, shape), in_specs=[hbm, hbm, hbm,...]
    unnamed x6 -> x4, local copies, waits for them, and re-layouts: 3.48 us -> 3.47 us
where the time goes in v2:
time: 146 us
  Pallas kernels  141 us (97%)
  local copies, waits for them, and re-layouts  3.47 us (2%)
  between operations  1.94 us (1%)
    pallas_call x1, Pallas kernels, per_device(): pl.pallas_call(kernel, out_shape=(shape, shape), in_specs=[hbm, hbm, hbm,...  141 us
    unnamed x4, local copies, waits for them, and re-layouts  3.47 us

profile of v2, /device:TPU:1, one launch (start us, length us, event | category | flops | bytes accessed | tf_op | source)
XLA Modules:
  0.0 146.1 jit_solution(18005732483610382883)
XLA Ops:
  1.9 140.7 %shard_map.95 = (bf16[192,3072]{1,0:T(8,128)(2,1)}, bf16[192,3072]{1,0:T(8,128)(2,1)}) custom-call(bf16[192,3072]{1,0:T(8,128)(2,1)} %bitcast.5, bf16[768,4608]{1,0:T(8,128)(2,1)} %w_hbm.1, bf16[384,3072]{1,0:T(8,128)(2,1)} %wo_hbm.1, bf16[256,2304]{1,0:T(8,128)(2,1)} %mw_hbm.1, s32[1]{0:T(128)S(6)} %copy.12.levels, s32[1]{0:T(128)S(6)} %copy.13.reach, ...), custom_call_target="tpu_custom_call" | custom-call | tf_op jit(solution)/shard_map/pallas_call | solution.py:553
  142.6 0.0 copy-start
  142.6 2.5 %copy.14 = bf16[2,96,3072]{2,1,0:T(8,128)(2,1)} copy(bf16[2,96,3072]{2,1,0:T(8,128)(2,1)} %bitcast.7) | data formatting | bytes 2359296
  145.1 0.0 copy-done
  145.1 1.0 copy.15
Async XLA Ops:
  142.6 2.5 %copy-start = (bf16[192,3072]{1,0:T(8,128)(2,1)S(1)}, bf16[192,3072]{1,0:T(8,128)(2,1)}, u32[]{:S(2)}) copy-start(bf16[192,3072]{1,0:T(8,128)(2,1)} %get-tuple-element.5) | copy-start | bytes 3538948

commit v3 on v2

--- a/solution.py
+++ b/solution.py
@@ -44,10 +44,12 @@
 BASE = {"z": [0] * 5, "y": [384] * ROUNDS + [0] * 2}
 AXES = [[axis for axis in "zy" if PIECE[axis][r]] for r in range(5)]
 WIDE = 3 * PAIR
+HALO_TIMES = [6.0, 6.01]
+NEXT_TIMES = [6.1, 6.11, 6.12, 6.13]
 
 
 def plan():
-    rate, latency, backlog, halo_time = 46500.0, 2.2, 2.2, 25.0
+    rate, latency, backlog, halo_time = 46500.0, 4.0, 100.0, 25.0
     busy, ready, arrivals, actions, work, waiting = {}, {}, [], [], [], []
 
     def cost(axis, r):
@@ -68,10 +70,12 @@
         for axis in AXES[r]:
             left[r] += 2 + sum(hops for key, hops in HOPS.items() if key[0] == axis)
             transmit("cross", 0.0, cost(axis, r), ("fetch", axis, r))
-    swaps = sum(len(axes) for axes in AXES)
     now = 6.0
-    transmit("cross", now, halo_time, ("halo",))
+    for time in HALO_TIMES + NEXT_TIMES:
+        what = ("halo send",) if time in HALO_TIMES else ("next send",)
+        heapq.heappush(arrivals, (time, 0, len(arrivals), what))
     halo = False
+    halos = 0
 
     def halo_work(r):
         return [("project", r, 1, False), ("project", r, 2, False), ("attend", r)]
@@ -79,8 +83,17 @@
     while True:
         if arrivals and arrivals[0][0] <= now:
             what = heapq.heappop(arrivals)[-1]
+            now += 0.05
+            if what[0] == "halo send":
+                actions.append(("halo send", halos))
+                halos += 1
+                if halos == len(HALO_TIMES):
+                    transmit("cross", now, halo_time, ("halo",))
+                continue
+            if what[0] == "next send":
+                actions.append(("next", len([0 for action in actions if action[0] == "next"])))
+                continue
             actions.append(("wait", *what))
-            now += 0.05
             if what[0] == "halo":
                 halo = True
                 work.append(("halo",))
@@ -114,9 +127,6 @@
                 sent = True
                 if item[0] == "swap":
                     transmit(link, now, cost(item[1], item[2]), item)
-                    swaps -= 1
-                    if swaps == 0:
-                        actions.append(("next",))
                 else:
                     kind, axis, way, half, k, r = item
                     transmit(link, now, cost(axis, r), (kind, axis, way, half, k + 1, r))
@@ -341,11 +351,21 @@
     send(mine, mine, ("hidden",), twin)
     halo_chip = jnp.where(c == 1, chip_after, chip_before)
     halo_base = jnp.where(c == 1, CHIP, CHIP + ROWS)
-    for core in range(2):
+
+    def halo_send(core):
         send(
             hidden.at[pl.ds(pl.multiple_of(own_rows + core * SPATIAL, 16), SPATIAL)],
             hidden.at[pl.ds(pl.multiple_of(halo_base + core * SPATIAL, 16), SPATIAL)],
             halo_key + 1 - c, (halo_chip, (1 - xh) * 2 + core),
+        )
+
+    def next_send(i):
+        core, part = i % 2, i // 2
+        rows = ROWS * 2 // len(NEXT_TIMES)
+        send(
+            x_hbm.at[pl.ds(part * rows, rows), pl.ds(core * INNER, INNER)],
+            next_x.at[pl.ds(pl.multiple_of(own_rows + part * rows, 16), rows)],
+            next_x_key + c, before[core],
         )
 
     def halo_forward():
@@ -452,12 +472,10 @@
                 send(region, region, ("swap", *rest), inner)
             else:
                 ring_send(*rest)
+        elif kind == "halo send":
+            halo_send(*rest)
         elif kind == "next":
-            for core in range(2):
-                send(
-                    x_hbm.at[:, pl.ds(core * INNER, INNER)], next_x.at[pl.ds(own_rows, ROWS)],
-                    next_x_key + c, before[core],
-                )
+            next_send(*rest)
         elif kind == "complete":
             complete(*rest)
             if first:

time: 146 us -> 139 us (0.952)
  Pallas kernels: 141 us -> 133 us
    pallas_call x1, Pallas kernels: 141 us -> 133 us  [per_device(): pl.pallas_call(kernel, out_shape=(shape, shape), in_specs=[hbm, hbm, hbm,...]
where the time goes in v3:
time: 139 us
  Pallas kernels  133 us (96%)
  local copies, waits for them, and re-layouts  3.47 us (2%)
  between operations  1.94 us (1%)
    pallas_call x1, Pallas kernels, per_device(): pl.pallas_call(kernel, out_shape=(shape, shape), in_specs=[hbm, hbm, hbm,...  133 us
    unnamed x4, local copies, waits for them, and re-layouts  3.47 us

profile of v3, /device:TPU:1, one launch (start us, length us, event | category | flops | bytes accessed | tf_op | source)
XLA Modules:
  0.0 138.5 jit_solution(6149470697906857844)
XLA Ops:
  1.9 133.1 %shard_map.95 = (bf16[192,3072]{1,0:T(8,128)(2,1)}, bf16[192,3072]{1,0:T(8,128)(2,1)}) custom-call(bf16[192,3072]{1,0:T(8,128)(2,1)} %bitcast.5, bf16[768,4608]{1,0:T(8,128)(2,1)} %w_hbm.1, bf16[384,3072]{1,0:T(8,128)(2,1)} %wo_hbm.1, bf16[256,2304]{1,0:T(8,128)(2,1)} %mw_hbm.1, s32[1]{0:T(128)S(6)} %copy.12.levels, s32[1]{0:T(128)S(6)} %copy.13.reach, ...), custom_call_target="tpu_custom_call" | custom-call | tf_op jit(solution)/shard_map/pallas_call | solution.py:571
  135.1 0.0 copy-start
  135.1 2.5 %copy.14 = bf16[2,96,3072]{2,1,0:T(8,128)(2,1)} copy(bf16[2,96,3072]{2,1,0:T(8,128)(2,1)} %bitcast.7) | data formatting | bytes 2359296
  137.5 0.0 copy-done
  137.5 1.0 copy.15
Async XLA Ops:
  135.1 2.5 %copy-start = (bf16[192,3072]{1,0:T(8,128)(2,1)S(1)}, bf16[192,3072]{1,0:T(8,128)(2,1)}, u32[]{:S(2)}) copy-start(bf16[192,3072]{1,0:T(8,128)(2,1)} %get-tuple-element.5) | copy-start | bytes 3538948

commit v4 on v2

--- a/solution.py
+++ b/solution.py
@@ -43,11 +43,14 @@
 PIECE = {"z": [48] * ROUNDS + [0] * 2, "y": [96] * ROUNDS + [96] * 2}
 BASE = {"z": [0] * 5, "y": [384] * ROUNDS + [0] * 2}
 AXES = [[axis for axis in "zy" if PIECE[axis][r]] for r in range(5)]
+DIRECT = ()
 WIDE = 3 * PAIR
+RELAY_TIMES = [18.0, 28.0]
+HALO_TIME = 36.0
 
 
 def plan():
-    rate, latency, backlog, halo_time = 46500.0, 2.2, 2.2, 25.0
+    rate, latency, backlog = 46500.0, 4.0, 100.0
     busy, ready, arrivals, actions, work, waiting = {}, {}, [], [], [], []
 
     def cost(axis, r):
@@ -67,10 +70,12 @@
     for r in range(5):
         for axis in AXES[r]:
             left[r] += 2 + sum(hops for key, hops in HOPS.items() if key[0] == axis)
-            transmit("cross", 0.0, cost(axis, r), ("fetch", axis, r))
-    swaps = sum(len(axes) for axes in AXES)
+            for what in ("fetch", "swap") if r in DIRECT else ("fetch",):
+                transmit("cross", 0.0, cost(axis, r), (what, axis, r))
     now = 6.0
-    transmit("cross", now, halo_time, ("halo",))
+    for i, time in enumerate(RELAY_TIMES):
+        heapq.heappush(arrivals, (time, 0, len(arrivals), ("relay", i)))
+    heapq.heappush(arrivals, (HALO_TIME, 0, len(arrivals), ("halo",)))
     halo = False
 
     def halo_work(r):
@@ -79,8 +84,11 @@
     while True:
         if arrivals and arrivals[0][0] <= now:
             what = heapq.heappop(arrivals)[-1]
+            now += 0.05
+            if what[0] == "relay":
+                actions.append(what)
+                continue
             actions.append(("wait", *what))
-            now += 0.05
             if what[0] == "halo":
                 halo = True
                 work.append(("halo",))
@@ -89,7 +97,7 @@
                 continue
             r = what[-1]
             left[r] -= 1
-            if what[0] == "fetch":
+            if what[0] == "fetch" and r not in DIRECT:
                 ready.setdefault("inner", []).append((r, 0, len(actions), ("swap", what[1], r)))
             if what[0] == "ring":
                 offer(*what[1:])
@@ -114,9 +122,6 @@
                 sent = True
                 if item[0] == "swap":
                     transmit(link, now, cost(item[1], item[2]), item)
-                    swaps -= 1
-                    if swaps == 0:
-                        actions.append(("next",))
                 else:
                     kind, axis, way, half, k, r = item
                     transmit(link, now, cost(axis, r), (kind, axis, way, half, k + 1, r))
@@ -138,7 +143,7 @@
     x_hbm, w_hbm, wo_hbm, mw_hbm, levels, reach, qgain, kgain,
     vel_hbm, next_hbm,
     weights, out_weights, hidden, own_x, half_x, next_x, mod_weights, part_mod, mod, shift, scale,
-    gate, next_gate, queries, keys, values, mixed, next_mixed, vel, stepped,
+    gate, next_gate, relay_rows, queries, keys, values, mixed, next_mixed, vel, stepped,
     send_sem, recv_sem, local_sem,
 ):
     f = lax.axis_index("frame")
@@ -165,10 +170,6 @@
     count = 64
     before = [((f + count - 1) % count, xh * 2 + core) for core in range(2)]
     after = [((f + 1) % count, xh * 2 + core) for core in range(2)]
-    chip_before = (f + count - 1 + xh) % count
-    chip_after = (f + xh) % count
-    halo = [(chip, (1 - xh) * 2 + core) for chip in (chip_before, chip_after) for core in range(2)]
-
     started = []
     numbers = {}
 
@@ -199,7 +200,10 @@
         locals_started.setdefault(key, []).append(copy)
 
     barrier = pltpu.get_barrier_semaphore()
-    greeted = [twin, inner, *cross, *ring.values(), *group, *before, *after, *halo]
+    passers = [(frame_of(y, z, 1 - xl), (1 - xh) * 2 + core) for core in range(2)]
+    around = [((f + count + way * step) % count, xh * 2 + core)
+              for way in (1, -1) for step in (1, 2) for core in range(2)]
+    greeted = [twin, inner, *passers, *ring.values(), *group, *around]
     for device in greeted:
         pl.semaphore_signal(barrier, inc=1, device_id=device, device_id_type=MESH)
 
@@ -256,11 +260,13 @@
 
     fetched = []
 
+    def direct(axis, r):
+        return direct_key + 4 * r + 2 * (axis == "z")
+
     def fetch(r):
         first = len(started)
 
-        @pl.when(c == 1 - xl)
-        def _():
+        def pieces():
             for axis in AXES[r]:
                 rows = PIECE[axis][r]
                 start = BASE[axis][r] + own[axis] * rows
@@ -270,8 +276,13 @@
                     for here, there in slabs(r, core):
                         send(
                             source(r).at[rows_here, here], buffers[r].at[rows_there, there],
-                            ("fetch", axis, r), cross[core],
+                            direct(axis, r) + jnp.where(c == 1 - xl, 0, 1), cross[core],
                         )
+
+        if r in DIRECT:
+            pieces()
+            return
+        pl.when(c == 1 - xl)(pieces)
 
         each = (len(started) - first) // len(AXES[r])
         for i in range(first, len(started)):
@@ -301,6 +312,15 @@
         for copy in locals_started.pop(r):
             copy.wait()
         received(buffers[r].at[shard_rows(r, xh * 2 + 1 - c)], ("twin", r))
+
+    def next_send(i):
+        core, part = i % 2, i // 2
+        rows = ROWS // 2
+        send(
+            x_hbm.at[pl.ds(part * rows, rows), pl.ds(core * INNER, INNER)],
+            next_x.at[pl.ds(pl.multiple_of(own_rows + part * rows, 16), rows)],
+            next_x_key + c, before[core],
+        )
 
     for device in group:
         send(part_mod, mod.at[m], mod_sem_key + m, device)
@@ -311,8 +331,9 @@
     )
     for r in range(5):
         exchange(r)
-    for r in range(2, 5):
-        fetch(r)
+    fetch(2)
+    for i in range(4):
+        next_send(i)
     for i in range(1, 4):
         owner = (m + i) % 4
         received(mod.at[owner], mod_sem_key + owner)
@@ -339,14 +360,37 @@
 
     mine = hidden.at[pl.ds(own_rows, ROWS)]
     send(mine, mine, ("hidden",), twin)
-    halo_chip = jnp.where(c == 1, chip_after, chip_before)
+    def halo_send(i):
+        frame = hidden.at[pl.ds(pl.multiple_of(own_rows + i * SPATIAL, 16), SPATIAL)]
+        passing = relay_rows.at[pl.ds(i * SPATIAL, SPATIAL)]
+        device = (frame_of(y, z, 1 - xl), (1 - xh) * 2 + c)
+        send(frame, passing, ("halo", i), device)
+
+    sender = frame_of(y, z, 1 - xl)
+    halo_frame = jnp.where(c == 1, sender + 1 - xh, sender + count - xh) % count
     halo_base = jnp.where(c == 1, CHIP, CHIP + ROWS)
-    for core in range(2):
-        send(
-            hidden.at[pl.ds(pl.multiple_of(own_rows + core * SPATIAL, 16), SPATIAL)],
-            hidden.at[pl.ds(pl.multiple_of(halo_base + core * SPATIAL, 16), SPATIAL)],
-            halo_key + 1 - c, (halo_chip, (1 - xh) * 2 + core),
-        )
+    passed = []
+
+    def relay(i):
+        passing = relay_rows.at[pl.ds(i * SPATIAL, SPATIAL)]
+        received(passing, ("halo", i))
+        device = (halo_frame, xh * 2 + i)
+        here = (halo_frame == f) & (c == i)
+        region = hidden.at[pl.ds(pl.multiple_of(halo_base + i * SPATIAL, 16), SPATIAL)]
+        place = len(started)
+        started.append(None)
+        passed.append((passing, here, place))
+
+        @pl.when(here)
+        def _():
+            pltpu.make_async_copy(passing, region, recv_sem.at[halo_key + 1 - c]).start()
+
+        @pl.when(jnp.logical_not(here))
+        def _():
+            pltpu.make_async_remote_copy(
+                src_ref=passing, dst_ref=region, send_sem=send_sem.at[place],
+                recv_sem=recv_sem.at[halo_key + 1 - c], device_id=device, device_id_type=MESH,
+            ).start()
 
     def halo_forward():
         for side in range(2):
@@ -432,15 +476,21 @@
             columns = pl.ds(pl.multiple_of((1 - c) * HALF + r * PAIR, PAIR), PAIR)
             received(buffer.at[:, columns], (name, r))
 
+    for i in range(2):
+        halo_send(i)
+    for r in range(3, 5):
+        fetch(r)
+
     first = True
     for action in plan():
         kind, rest = action[0], action[1:]
         if kind == "wait":
             kind, rest = rest[0], rest[1:]
             if kind == "fetch":
-                received(piece(rest[0], shard_of["a"], own[rest[0]], rest[1]), ("fetch", *rest))
+                received(piece(rest[0], shard_of["a"], own[rest[0]], rest[1]), direct(*rest))
             elif kind == "swap":
-                received(piece(rest[0], shard_of["b"], own[rest[0]], rest[1]), ("swap", *rest))
+                key = direct(*rest) + 1 if rest[1] in DIRECT else ("swap", *rest)
+                received(piece(rest[0], shard_of["b"], own[rest[0]], rest[1]), key)
             elif kind == "ring":
                 arrived(*rest)
             else:
@@ -452,12 +502,8 @@
                 send(region, region, ("swap", *rest), inner)
             else:
                 ring_send(*rest)
-        elif kind == "next":
-            for core in range(2):
-                send(
-                    x_hbm.at[:, pl.ds(core * INNER, INNER)], next_x.at[pl.ds(own_rows, ROWS)],
-                    next_x_key + c, before[core],
-                )
+        elif kind == "relay":
+            relay(*rest)
         elif kind == "complete":
             complete(*rest)
             if first:
@@ -527,6 +573,14 @@
         if copy is not None:
             copy.wait_send()
 
+    for passing, here, place in passed:
+        pl.when(jnp.logical_not(here))(
+            pltpu.make_async_remote_copy(
+                src_ref=passing, dst_ref=passing, send_sem=send_sem.at[place],
+                recv_sem=recv_sem.at[0], device_id=twin, device_id_type=MESH,
+            ).wait_send
+        )
+
     @pl.when(c == 1 - xl)
     def _():
         for region, i in fetched:
@@ -539,7 +593,8 @@
 mod_sem_key = 160
 halo_key = 164
 next_x_key = 166
-SEMAPHORES = 168
+direct_key = 168
+SEMAPHORES = 188
 SENDS = 288
 
 
@@ -569,6 +624,7 @@
             pltpu.VMEM((1, D), F32),
             pltpu.VMEM((1, D + HEAD), F32),
             pltpu.VMEM((1, D + HEAD), F32),
+            pltpu.VMEM((ROWS, D), BF16),
             pltpu.VMEM((ROUNDS, CHIP, PAIR), BF16),
             pltpu.VMEM((ROUNDS, 2 * CHIP, PAIR), BF16),
             pltpu.VMEM((ROUNDS, 2 * CHIP, PAIR), BF16),

time: 146 us -> 132 us (0.904); the launches traced: 146 us -> 130 us
  Pallas kernels: 141 us -> 124 us
    pallas_call x1, Pallas kernels: 141 us -> 124 us  [per_device(): pl.pallas_call(kernel, out_shape=(shape, shape), in_specs=[hbm, hbm, hbm,...]
where the time goes in v4:
time: 132 us; the launch traced here: 130 us
  Pallas kernels  124 us (94%)
  local copies, waits for them, and re-layouts  3.47 us (3%)
  between operations  1.94 us (1%)
    pallas_call x1, Pallas kernels, per_device(): pl.pallas_call(kernel, out_shape=(shape, shape), in_specs=[hbm, hbm, hbm,...  124 us
    unnamed x4, local copies, waits for them, and re-layouts  3.47 us

profile of v4, /device:TPU:1, one launch (start us, length us, event | category | flops | bytes accessed | tf_op | source)
XLA Modules:
  0.0 129.6 jit_solution(13526843043248471442)
XLA Ops:
  1.9 124.2 %shard_map.95 = (bf16[192,3072]{1,0:T(8,128)(2,1)}, bf16[192,3072]{1,0:T(8,128)(2,1)}) custom-call(bf16[192,3072]{1,0:T(8,128)(2,1)} %bitcast.5, bf16[768,4608]{1,0:T(8,128)(2,1)} %w_hbm.1, bf16[384,3072]{1,0:T(8,128)(2,1)} %wo_hbm.1, bf16[256,2304]{1,0:T(8,128)(2,1)} %mw_hbm.1, s32[1]{0:T(128)S(6)} %copy.12.levels, s32[1]{0:T(128)S(6)} %copy.13.reach, ...), custom_call_target="tpu_custom_call" | custom-call | tf_op jit(solution)/shard_map/pallas_call | solution.py:608
  126.1 0.0 copy-start
  126.1 2.5 %copy.14 = bf16[2,96,3072]{2,1,0:T(8,128)(2,1)} copy(bf16[2,96,3072]{2,1,0:T(8,128)(2,1)} %bitcast.7) | data formatting | bytes 2359296
  128.6 0.0 copy-done
  128.6 1.0 copy.15
Async XLA Ops:
  126.1 2.5 %copy-start = (bf16[192,3072]{1,0:T(8,128)(2,1)S(1)}, bf16[192,3072]{1,0:T(8,128)(2,1)}, u32[]{:S(2)}) copy-start(bf16[192,3072]{1,0:T(8,128)(2,1)} %get-tuple-element.5) | copy-start | bytes 3538948
